TPU v7x, 128 devices: a whole 4x4x4 slice. The times are simulated.
128 devices in a mesh: pair: 16 (over z, y), virt: 8 (over x, core).
Axes of the slice: x: 4, y: 4, z: 4, core: 2. Of those that a mesh axis runs over, the one named last changes fastest.
Arguments:
- amplitudes: bfloat16 [1024, 32768], P('pair', 'virt'), may hold values from -6 to 6
- ladder_ints: bfloat16 [32768, 8, 4096], P('virt', None, 'pair'), may hold values from -0.09375 to 0.09375
- hole_ints: bfloat16 [1024, 1024], P('pair'), may hold values from -0.1875 to 0.1875
- tile_irrep: int32 [256], replicated, may hold values from 0 to 7, as said below
- pair_orbitals: int32 [1024, 2], P('pair'), may hold values from 0 to 199
- occ_energy: float32 [200], replicated, may hold values from -3 to -0.3
- pair_energy: float32 [32768], P('virt'), may hold values from 0.5 to 4
Outputs:
- residual: float32 [1024, 32768], P('pair', 'virt')
- update: bfloat16 [1024, 32768], P('pair', 'virt')
Inputs may be any that keep to these rules, and one draw needn't show every extreme that they name: `tile_irrep`: each aligned block of 8 consecutive tiles holds every label exactly once.
All inputs are finite; a program needn't handle non-finite values.
Results may differ from a plain program's by a relative error of at most 0.001.
Values may be sent and summed in bfloat16 or wider, within the bound.
No kernel may reach another device: no remote copies, remote signals or barrier semaphores. Data moves between devices by JAX's collectives and lax.ppermute only.
A program may use at most 192 MiB of HBM per device.

v0:
```python
import jax
import jax.numpy as jnp
from jax import lax
from jax.sharding import PartitionSpec as P

TW = 128


def local(amplitudes, ladder_ints, hole_ints, tile_irrep, pair_orbitals, occ_energy, pair_energy):
    rows_cd = ladder_ints.shape[0]
    outer = ladder_ints.shape[1]
    inner = ladder_ints.shape[2]
    pairs = hole_ints.shape[1]
    local_pairs = amplitudes.shape[0]
    virt_pos = lax.axis_index("virt")
    pair_pos = lax.axis_index("pair")
    cd_tiles = rows_cd // TW
    ab_tiles = inner // TW
    cd_irrep = lax.dynamic_slice_in_dim(tile_irrep, virt_pos * cd_tiles, cd_tiles, 0)
    label_grid = tile_irrep.reshape(outer, cd_tiles)
    ab_irrep = lax.dynamic_slice_in_dim(label_grid, pair_pos * ab_tiles, ab_tiles, 1)
    tile_mask = (cd_irrep[:, None, None] == ab_irrep[None, :, :]).astype(ladder_ints.dtype)
    masked = (
        ladder_ints.reshape(cd_tiles, TW, outer, ab_tiles, TW) * tile_mask[:, None, :, :, None]
    ).reshape(rows_cd, outer * inner)
    piece = lax.all_gather(amplitudes, "pair", axis=0, tiled=True)
    ladder = jnp.dot(piece, masked, preferred_element_type=jnp.float32)
    hole = jnp.dot(hole_ints, piece, preferred_element_type=jnp.float32)
    ladder, hole = (ladder, hole)
    regrouped = lax.all_to_all(
        ladder.reshape(pairs, outer, inner), "pair", split_axis=0, concat_axis=2, tiled=True
    )
    particle = lax.psum_scatter(regrouped, "virt", scatter_dimension=1, tiled=True)
    residual = particle.reshape(local_pairs, rows_cd) + hole
    orbital_range = jnp.arange(occ_energy.shape[0], dtype=jnp.int32)
    onehot = (pair_orbitals[:, :, None] == orbital_range[None, None, :]).astype(jnp.float32)
    occupied = jnp.sum(onehot * occ_energy[None, None, :], axis=(1, 2))
    denom = pair_energy[None, :] - occupied[:, None]
    update = (residual / denom).astype(jnp.bfloat16)
    return (residual, update)


def solution(mesh):
    placed = (
        P("pair", "virt"),
        P("virt", None, "pair"),
        P("pair", None),
        P(),
        P("pair", None),
        P(),
        P("virt"),
    )
    return jax.shard_map(
        local,
        mesh=mesh,
        in_specs=placed,
        out_specs=(P("pair", "virt"), P("pair", "virt")),
        check_vma=False,
    )
```

profile of v0, /device:TPU:1, one launch (start us, length us, event | category | flops | bytes accessed | tf_op | source)
XLA Modules:
  0.0 300.2 jit_solution(4230927393608967305)
XLA Ops:
  7.2 0.0 copy-start
  7.2 0.0 all-gather.2.cloned.1.call-start
  7.2 0.7 all-gather.2.cloned.1.call-update
  7.9 0.0 reduce-scatter.2.cloned.1.call-start
  8.0 0.8 reshape.28
  8.7 0.8 dynamic_slice.6
  9.5 0.1 constant_dynamic-slice_fusion
  9.5 0.1 compare_convert_fusion
  9.7 12.2 %mul.27 = bf16[32,128,8,2,128]{4,3,2,1,0:T(2,128)(2,1)} broadcast(bf16[32,8,2]{2,1,0:T(8,128)(2,1)S(1)} %compare_convert_fusion), dimensions={0,2,3} | broadcast | bytes 16778240 | tf_op jit(solution)/shard_map/mul | solution.py:24
  21.8 28.0 %mul.28 = bf16[4096,2048]{1,0:T(8,128)(2,1)} reshape(bf16[32,128,8,2,128]{4,3,2,1,0:T(2,128)(2,1)} %mul.27) | data formatting | bytes 33554432 | tf_op jit(solution)/shard_map/mul | solution.py:24
  49.8 16.3 %copy.16 = bf16[512,8,8,256]{3,1,2,0:T(8,128)(2,1)} copy(bf16[512,8,8,256]{3,2,1,0:T(8,128)(2,1)} %bitcast.18) | data formatting | bytes 33554432
  66.1 18.2 %all-gather.2.cloned.1.call-done = bf16[1024,4096]{1,0:T(8,128)(2,1)} async-done(((bf16[64,4096]{1,0:T(8,128)(2,1)}), bf16[1024,4096]{1,0:T(8,128)(2,1)}) %all-gather.2.cloned.1.call-update) | async-done | bytes 8388624 | tf_op jit(solution)/shard_map/all_gather | solution.py:26
  84.3 25.4 %fusion = f32[2048,1024]{1,0:T(8,128)} fusion(bf16[1024,4096]{1,0:T(8,128)(2,1)} %all-gather.2.cloned.1.call-done, bf16[4096,2048]{1,0:T(8,128)(2,1)} %bitcast.19, bf16[4096,2048]{1,0:T(8,128)(2,1)} %mul.28), kind=kOutput, calls=%fused_computation | convolution fusion | flops 17188257792 | bytes 50331648 | tf_op jit(solution)/shard_map/dot_general | solution.py:27
  109.7 9.3 %copy.14 = f32[1024,8,256]{2,1,0:T(8,128)} copy(f32[1024,8,256]{0,2,1:T(8,128)} %bitcast.20) | data formatting | bytes 16777216 | tf_op jit(solution)/shard_map/reshape | solution.py:31
  119.0 99.8 %all_to_all.18 = f32[1024,8,256]{2,1,0:T(8,128)S(1)} all-to-all(f32[1024,8,256]{2,1,0:T(8,128)} %copy.14), channel_id=1, replica_groups=mesh['pair'=16,'virt'=8] {'pair'}, dimensions={0} | all-to-all | bytes 16777216 | tf_op jit(solution)/shard_map/all_to_all | solution.py:30
  218.8 8.1 %copy.15 = f32[64,8,16,256]{3,2,0,1:T(8,128)} copy(f32[64,8,16,256]{3,1,0,2:T(8,128)S(1)} %bitcast.17) | data formatting | bytes 16777216 | tf_op jit(solution)/shard_map/all_to_all | solution.py:30
  226.8 9.4 %all_to_all.16 = f32[64,8,4096]{2,0,1:T(8,128)} reshape(f32[64,8,16,256]{3,2,0,1:T(8,128)} %copy.15) | data formatting | bytes 16777216 | tf_op jit(solution)/shard_map/all_to_all | solution.py:30
  236.2 0.0 copy-start.2
  236.2 0.0 copy-start.3
  236.2 0.0 copy-start.1
  236.2 0.0 reduce-scatter.2.cloned.1.call-update
  236.3 0.6 copy-done.2
  236.9 0.0 copy-done.3
  236.9 0.2 select_reduce_fusion
  237.1 49.9 %reduce-scatter.2.cloned.1.call-done = f32[64,1,4096]{2,0,1:T(8,128)} async-done(((f32[64,8,4096]{2,0,1:T(8,128)}), f32[64,1,4096]{2,0,1:T(8,128)}) %reduce-scatter.2.cloned.1.call-update) | async-done | bytes 1048592 | tf_op jit(solution)/shard_map/reduce_scatter | solution.py:33
  287.0 0.0 copy-done
  287.0 0.0 copy-done.1
  287.0 6.3 %divide_convert_fusion = (bf16[64,4096]{1,0:T(8,128)(2,1)}, f32[64,4096]{1,0:T(8,128)}) fusion(f32[64]{0:T(128)S(1)} %select_reduce_fusion, f32[4096]{0:T(1024)S(1)} %copy-done.1, bf16[64,1024]{1,0:T(8,128)(2,1)S(1)} %copy-done, bf16[1024,4096]{1,0:T(8,128)(2,1)} %all-gather.2.cloned.1.call-done, f32[64,1,4096]{2,0,1:T(8,128)} %reduce-scatter.2.cloned.1.call-done), kind=kOutput, calls=%fused_computation.3 | convolution fusion | flops 537919488 | bytes 11157760 | tf_op jit(solution)/shard_map/dot_general | solution.py:28
Async XLA Ops:
  7.2 279.8 %copy-start = (bf16[64,1024]{1,0:T(8,128)(2,1)S(1)}, bf16[64,1024]{1,0:T(8,128)(2,1)}, u32[]{:S(2)}) copy-start(bf16[64,1024]{1,0:T(8,128)(2,1)} %param.9) | copy-start | bytes 393220
  7.2 77.1 %all-gather.2.cloned.1.call-start = ((), (), s32[]{:S(2)}) async-start(), calls=%async_computation.2 | async-start | bytes 8912896 | tf_op jit(solution)/shard_map/all_gather | solution.py:26
  7.9 279.1 %reduce-scatter.2.cloned.1.call-start = ((), (), s32[]{:S(2)}) async-start(), calls=%async_computation.3 | async-start | bytes 9437184 | tf_op jit(solution)/shard_map/reduce_scatter | solution.py:33
  236.2 0.7 copy-start.2
  236.2 0.7 copy-start.3
  236.2 50.8 %copy-start.1 = (f32[4096]{0:T(1024)S(1)}, f32[4096]{0:T(1024)}, u32[]{:S(2)}) copy-start(f32[4096]{0:T(1024)} %param.13) | copy-start | bytes 49156
Sparse Core Ops, SparseCore 0:
  10.2 74.0 all-gather.1
  236.4 50.5 reduce-scatter.1
where the time goes:
time: 302 us; the launch traced here: 300 us
  blocking collectives  99.8 us (33%)
  local copies, waits for them, and re-layouts  85.4 us (28%)
  waiting for transfers between devices  68.8 us (23%)
  matrix products  31.8 us (11%)
  between operations  14.1 us (5%)
    all_to_all x1, blocking collectives, local(): lax.all_to_all(ladder.reshape(pairs, outer, inner), 'pair', split_axis=0,...  99.8 us
    reduce_scatter x1, waiting for transfers between devices, local(): lax.psum_scatter(regrouped, 'virt', scatter_dimension=1, tiled=True)  49.9 us
    mul x2, local copies, waits for them, and re-layouts, local(): ladder_ints.reshape(cd_tiles, TW, outer, ab_tiles, TW)  40.1 us
    dot_general x1, matrix products, local(): ladder = jnp.dot(piece, masked, preferred_element_type=jnp.float32)  25.4 us
    all_gather x1, waiting for transfers between devices, local(): piece = lax.all_gather(amplitudes, 'pair', axis=0, tiled=True)  18.2 us
    all_to_all x2, local copies, waits for them, and re-layouts, local(): lax.all_to_all(ladder.reshape(pairs, outer, inner), 'pair', split_axis=0,...  17.5 us
    unnamed x9, local copies, waits for them, and re-layouts  17 us
    reshape x1, local copies, waits for them, and re-layouts, local(): ladder.reshape(pairs, outer, inner)  9.28 us
  transfers between devices with their start and end apart: 2, of which 2 were waited for; matrix products, arithmetic and copies ran while one was open for 19% of the time, Pallas kernels for 0%

commit v1 on v0

--- a/solution.py
+++ b/solution.py
@@ -27,8 +27,16 @@
     ladder = jnp.dot(piece, masked, preferred_element_type=jnp.float32)
     hole = jnp.dot(hole_ints, piece, preferred_element_type=jnp.float32)
     ladder, hole = (ladder, hole)
-    regrouped = lax.all_to_all(
-        ladder.reshape(pairs, outer, inner), "pair", split_axis=0, concat_axis=2, tiled=True
+    regrouped = jnp.concatenate(
+        lax.all_to_all(
+            jnp.stack(
+                jnp.split(ladder.reshape(pairs, outer, inner), lax.axis_size("pair"), axis=0)
+            ),
+            "pair",
+            0,
+            0,
+        ),
+        axis=2,
     )
     particle = lax.psum_scatter(regrouped, "virt", scatter_dimension=1, tiled=True)
     residual = particle.reshape(local_pairs, rows_cd) + hole

time: 302 us -> 295 us (0.977)
  local copies, waits for them, and re-layouts: 85.4 us -> 80.4 us
    all_to_all x2 -> x0, local copies, waits for them, and re-layouts: 17.5 us -> none  [local(): lax.all_to_all(ladder.reshape(pairs, outer, inner), 'pair', split_axis=0,...]
    reshape x1 -> x2, local copies, waits for them, and re-layouts: 9.28 us -> 17.5 us  [local(): jnp.concatenate(lax.all_to_all(jnp.stack(jnp.split(ladder.reshape(pairs,...]
    unnamed x9 -> x40, local copies, waits for them, and re-layouts: 17 us -> 20.1 us
  transfers between devices with their start and end apart: 2 -> 2, of which waited for: 2 -> 2; matrix products, arithmetic and copies ran while one was open for 19% -> 20% of each run, Pallas kernels for 0% -> 0%
where the time goes in v1:
time: 295 us; the launch traced here: 294 us
  blocking collectives  99.6 us (34%)
  local copies, waits for them, and re-layouts  80.4 us (27%)
  waiting for transfers between devices  68.8 us (23%)
  matrix products  30.3 us (10%)
  between operations  14.3 us (5%)
    all_to_all x1, blocking collectives, local(): lax.all_to_all(jnp.stack(jnp.split(ladder.reshape(pairs, outer, inner), l...  99.6 us
    reduce_scatter x1, waiting for transfers between devices, local(): lax.psum_scatter(regrouped, 'virt', scatter_dimension=1, tiled=True)  49.9 us
    mul x2, local copies, waits for them, and re-layouts, local(): ladder_ints.reshape(cd_tiles, TW, outer, ab_tiles, TW)  40.1 us
    dot_general x1, matrix products, local(): ladder = jnp.dot(piece, masked, preferred_element_type=jnp.float32)  23.9 us
    unnamed x40, local copies, waits for them, and re-layouts  20.1 us
    all_gather x1, waiting for transfers between devices, local(): piece = lax.all_gather(amplitudes, 'pair', axis=0, tiled=True)  18.2 us
    reshape x2, local copies, waits for them, and re-layouts, local(): jnp.concatenate(lax.all_to_all(jnp.stack(jnp.split(ladder.reshape(pairs,...  17.5 us
    dot_general x1, matrix products, local(): hole = jnp.dot(hole_ints, piece, preferred_element_type=jnp.float32)  6.35 us
  transfers between devices with their start and end apart: 2, of which 2 were waited for; matrix products, arithmetic and copies ran while one was open for 20% of the time, Pallas kernels for 0%

profile of v1, /device:TPU:1, one launch (start us, length us, event | category | flops | bytes accessed | tf_op | source)
XLA Modules:
  0.0 293.7 jit_solution(12980953858050897887)
XLA Ops:
  7.2 0.0 copy-start
  7.2 0.0 all-gather.2.cloned.1.call-start
  7.2 0.7 all-gather.2.cloned.1.call-update
  7.9 0.0 reduce-scatter.2.cloned.1.call-start
  8.0 0.8 reshape.64
  8.7 0.8 dynamic_slice.6
  9.5 0.1 constant_dynamic-slice_fusion
  9.5 0.1 compare_convert_fusion
  9.7 12.2 %mul.27 = bf16[32,128,8,2,128]{4,3,2,1,0:T(2,128)(2,1)} broadcast(bf16[32,8,2]{2,1,0:T(8,128)(2,1)S(1)} %compare_convert_fusion), dimensions={0,2,3} | broadcast | bytes 16778240 | tf_op jit(solution)/shard_map/mul | solution.py:24
  21.8 28.0 %mul.28 = bf16[4096,2048]{1,0:T(8,128)(2,1)} reshape(bf16[32,128,8,2,128]{4,3,2,1,0:T(2,128)(2,1)} %mul.27) | data formatting | bytes 33554432 | tf_op jit(solution)/shard_map/mul | solution.py:24
  49.8 16.3 %copy.12 = bf16[512,8,8,256]{3,1,2,0:T(8,128)(2,1)} copy(bf16[512,8,8,256]{3,2,1,0:T(8,128)(2,1)} %bitcast.95) | data formatting | bytes 33554432
  66.1 18.2 %all-gather.2.cloned.1.call-done = bf16[1024,4096]{1,0:T(8,128)(2,1)} async-done(((bf16[64,4096]{1,0:T(8,128)(2,1)}), bf16[1024,4096]{1,0:T(8,128)(2,1)}) %all-gather.2.cloned.1.call-update) | async-done | bytes 8388624 | tf_op jit(solution)/shard_map/all_gather | solution.py:26
  84.3 23.9 %fusion.2 = f32[1024,2048]{1,0:T(8,128)S(1)} fusion(bf16[1024,4096]{1,0:T(8,128)(2,1)} %all-gather.2.cloned.1.call-done, bf16[4096,2048]{1,0:T(8,128)(2,1)} %bitcast.96, bf16[4096,2048]{1,0:T(8,128)(2,1)} %mul.28), kind=kOutput, calls=%fused_computation.3 | convolution fusion | flops 17188257792 | bytes 50331648 | tf_op jit(solution)/shard_map/dot_general | solution.py:27
  108.2 1.0 fusion.5
  109.2 0.2 copy.13
  109.5 0.2 copy.14
  109.6 0.2 copy.15
  109.8 0.2 copy.16
  110.0 0.2 copy.17
  110.1 0.2 copy.18
  110.3 0.2 copy.19
  110.5 0.2 copy.20
  110.7 0.2 copy.21
  110.8 0.2 copy.22
  111.0 0.2 copy.23
  111.2 0.2 copy.24
  111.3 0.2 copy.25
  111.5 0.2 copy.26
  111.7 0.2 copy.27
  111.8 0.2 copy.28
  112.7 99.6 %all_to_all.5 = f32[16,64,8,256]{3,2,1,0:T(8,128)S(1)} all-to-all(f32[16,64,8,256]{3,2,1,0:T(8,128)S(1)} %bitcast_dynamic-update-slice_fusion), channel_id=1, replica_groups=mesh['pair'=16,'virt'=8] {'pair'}, dimensions={0} | all-to-all | bytes 16777216 | tf_op jit(solution)/shard_map/all_to_all | solution.py:31
  212.3 8.1 %copy.11 = f32[64,8,16,256]{3,2,0,1:T(8,128)} copy(f32[64,8,16,256]{3,1,0,2:T(8,128)S(1)} %bitcast.94) | data formatting | bytes 16777216 | tf_op jit(solution)/shard_map/reshape | solution.py:30
  220.3 9.4 %reshape.66 = f32[64,8,4096]{2,0,1:T(8,128)} reshape(f32[64,8,16,256]{3,2,0,1:T(8,128)} %copy.11) | data formatting | bytes 16777216 | tf_op jit(solution)/shard_map/reshape | solution.py:30
  229.7 0.0 copy-start.2
  229.7 0.0 copy-start.3
  229.7 0.0 copy-start.1
  229.7 0.0 reduce-scatter.2.cloned.1.call-update
  229.8 0.6 copy-done.2
  230.4 0.0 copy-done.3
  230.4 0.2 select_reduce_fusion
  230.6 49.9 %reduce-scatter.2.cloned.1.call-done = f32[64,1,4096]{2,0,1:T(8,128)} async-done(((f32[64,8,4096]{2,0,1:T(8,128)}), f32[64,1,4096]{2,0,1:T(8,128)}) %reduce-scatter.2.cloned.1.call-update) | async-done | bytes 1048592 | tf_op jit(solution)/shard_map/reduce_scatter | solution.py:41
  280.5 0.0 copy-done
  280.5 0.0 copy-done.1
  280.5 6.3 %divide_convert_fusion = (bf16[64,4096]{1,0:T(8,128)(2,1)}, f32[64,4096]{1,0:T(8,128)}) fusion(f32[64]{0:T(128)S(1)} %select_reduce_fusion, f32[4096]{0:T(1024)S(1)} %copy-done.1, bf16[64,1024]{1,0:T(8,128)(2,1)S(1)} %copy-done, bf16[1024,4096]{1,0:T(8,128)(2,1)} %all-gather.2.cloned.1.call-done, f32[64,1,4096]{2,0,1:T(8,128)} %reduce-scatter.2.cloned.1.call-done), kind=kOutput, calls=%fused_computation.4 | convolution fusion | flops 537919488 | bytes 11157760 | tf_op jit(solution)/shard_map/dot_general | solution.py:28
  (16 shorter events, 0.6 us)
Async XLA Ops:
  7.2 273.4 %copy-start = (bf16[64,1024]{1,0:T(8,128)(2,1)S(1)}, bf16[64,1024]{1,0:T(8,128)(2,1)}, u32[]{:S(2)}) copy-start(bf16[64,1024]{1,0:T(8,128)(2,1)} %param.9) | copy-start | bytes 393220
  7.2 77.1 %all-gather.2.cloned.1.call-start = ((), (), s32[]{:S(2)}) async-start(), calls=%async_computation.2 | async-start | bytes 8912896 | tf_op jit(solution)/shard_map/all_gather | solution.py:26
  7.9 272.6 %reduce-scatter.2.cloned.1.call-start = ((), (), s32[]{:S(2)}) async-start(), calls=%async_computation.3 | async-start | bytes 9437184 | tf_op jit(solution)/shard_map/reduce_scatter | solution.py:41
  229.7 0.7 copy-start.2
  229.7 0.7 copy-start.3
  229.7 50.8 %copy-start.1 = (f32[4096]{0:T(1024)S(1)}, f32[4096]{0:T(1024)}, u32[]{:S(2)}) copy-start(f32[4096]{0:T(1024)} %param.13) | copy-start | bytes 49156
Sparse Core Ops, SparseCore 0:
  10.2 74.0 all-gather.1
  229.9 50.5 reduce-scatter.1

commit v2 on v0

--- a/solution.py
+++ b/solution.py
@@ -23,7 +23,9 @@
     masked = (
         ladder_ints.reshape(cd_tiles, TW, outer, ab_tiles, TW) * tile_mask[:, None, :, :, None]
     ).reshape(rows_cd, outer * inner)
-    piece = lax.all_gather(amplitudes, "pair", axis=0, tiled=True)
+    piece = jnp.concatenate(
+        lax.all_to_all(jnp.stack([amplitudes] * lax.axis_size("pair")), "pair", 0, 0), axis=0
+    )
     ladder = jnp.dot(piece, masked, preferred_element_type=jnp.float32)
     hole = jnp.dot(hole_ints, piece, preferred_element_type=jnp.float32)
     ladder, hole = (ladder, hole)

time: 302 us -> 362 us (1.20)
  waiting for transfers between devices: 68.8 us -> 151 us
  local copies, waits for them, and re-layouts: 85.4 us -> 45.6 us
  other arithmetic: 0.28 us -> 9.92 us
  starting transfers between devices: 0.08 us -> 8.82 us
    all_to_all x0 -> x1, waiting for transfers between devices: none -> 100 us  [local(): lax.all_to_all(jnp.stack([amplitudes] * lax.axis_size('pair')), 'pair', 0...]
    mul x2 -> x1, local copies, waits for them, and re-layouts: 40.1 us -> 2.8 us  [local(): ladder_ints.reshape(cd_tiles, TW, outer, ab_tiles, TW)]
    all_gather x1 -> x0, waiting for transfers between devices: 18.2 us -> none  [local(): piece = lax.all_gather(amplitudes, 'pair', axis=0, tiled=True)]
    mul x0 -> x1, other arithmetic: none -> 9.64 us  [local(): ladder_ints.reshape(cd_tiles, TW, outer, ab_tiles, TW)]
    all_to_all x0 -> x1, starting transfers between devices: none -> 8.78 us  [local(): lax.all_to_all(jnp.stack([amplitudes] * lax.axis_size('pair')), 'pair', 0...]
    unnamed x9 -> x11, local copies, waits for them, and re-layouts: 17 us -> 10.4 us
    another operation x0 -> x1, local copies, waits for them, and re-layouts: none -> 5.37 us  [local(): jnp.stack([amplitudes] * lax.axis_size('pair'))]
  transfers between devices with their start and end apart: 2 -> 2, of which waited for: 2 -> 2; matrix products, arithmetic and copies ran while one was open for 19% -> 6% of each run, Pallas kernels for 0% -> 0%
where the time goes in v2:
time: 362 us; the launch traced here: 361 us
  waiting for transfers between devices  151 us (42%)
  blocking collectives  101 us (28%)
  local copies, waits for them, and re-layouts  45.6 us (13%)
  matrix products  30.6 us (8%)
  between operations  14.1 us (4%)
  other arithmetic  9.92 us (3%)
  starting transfers between devices  8.82 us (2%)
    all_to_all x1, blocking collectives, local(): lax.all_to_all(ladder.reshape(pairs, outer, inner), 'pair', split_axis=0,...  101 us
    all_to_all x1, waiting for transfers between devices, local(): lax.all_to_all(jnp.stack([amplitudes] * lax.axis_size('pair')), 'pair', 0...  100 us
    reduce_scatter x1, waiting for transfers between devices, local(): lax.psum_scatter(regrouped, 'virt', scatter_dimension=1, tiled=True)  50.6 us
    dot_general x1, matrix products, local(): ladder = jnp.dot(piece, masked, preferred_element_type=jnp.float32)  24.2 us
    all_to_all x2, local copies, waits for them, and re-layouts, local(): lax.all_to_all(ladder.reshape(pairs, outer, inner), 'pair', split_axis=0,...  17.5 us
    unnamed x11, local copies, waits for them, and re-layouts  10.4 us
    mul x1, other arithmetic, local(): ladder_ints.reshape(cd_tiles, TW, outer, ab_tiles, TW)  9.64 us
    reshape x1, local copies, waits for them, and re-layouts, local(): ladder.reshape(pairs, outer, inner)  9.28 us
  transfers between devices with their start and end apart: 2, of which 2 were waited for; matrix products, arithmetic and copies ran while one was open for 6% of the time, Pallas kernels for 0%

profile of v2, /device:TPU:1, one launch (start us, length us, event | category | flops | bytes accessed | tf_op | source)
XLA Modules:
  0.0 361.4 jit_solution(8499899430939547207)
XLA Ops:
  7.2 0.0 copy-start
  7.2 5.4 %stack.2 = bf16[16,64,4096]{2,1,0:T(8,128)(2,1)} broadcast(bf16[64,4096]{1,0:T(8,128)(2,1)} %param.7), dimensions={1,2} | broadcast | bytes 8912896 | tf_op jit(solution)/shard_map/stack | solution.py:27
  12.5 0.0 copy-start.2
  12.5 8.8 %all-to-all-start = ((bf16[16,64,4096]{2,1,0:T(8,128)(2,1)}), bf16[16,64,4096]{2,1,0:T(8,128)(2,1)}, u32[]{:S(2)}, u32[]{:S(2)}) async-start(bf16[16,64,4096]{2,1,0:T(8,128)(2,1)} %stack.2), calls=%async_computation | async-start | bytes 16777216 | tf_op jit(solution)/shard_map/all_to_all | solution.py:27
  21.3 0.0 reduce-scatter.2.cloned.1.call-start
  21.4 0.0 copy-done.2
  21.4 0.1 reshape.32
  21.5 0.1 constant_dynamic-slice_fusion
  21.6 0.1 copy.15
  21.6 0.1 dynamic_slice.6
  21.7 0.1 compare_convert_fusion
  21.8 2.8 mul.30
  24.6 9.6 %mul.32 = bf16[4096,8,256]{2,1,0:T(8,128)(2,1)S(1)} multiply(bf16[4096,8,256]{2,1,0:T(8,128)(2,1)} %param.8, bf16[4096,8,256]{2,1,0:T(8,128)(2,1)S(1)} %bitcast.20) | non-fusion elementwise | flops 8388608 | bytes 50331648 | tf_op jit(solution)/shard_map/mul | solution.py:24
  34.3 9.7 %copy.18 = bf16[512,8,8,256]{3,1,2,0:T(8,128)(2,1)} copy(bf16[512,8,8,256]{3,2,1,0:T(8,128)(2,1)S(1)} %bitcast.21) | data formatting | bytes 33554432
  44.0 100.5 %all-to-all-done = bf16[16,64,4096]{2,1,0:T(8,128)(2,1)} async-done(((bf16[16,64,4096]{2,1,0:T(8,128)(2,1)}), bf16[16,64,4096]{2,1,0:T(8,128)(2,1)}, u32[]{:S(2)}, u32[]{:S(2)}) %all-to-all-start) | async-done | bytes 8388640 | tf_op jit(solution)/shard_map/all_to_all | solution.py:27
  144.5 24.2 %fusion = f32[2048,1024]{1,0:T(8,128)} fusion(bf16[4096,2048]{1,0:T(8,128)(2,1)} %bitcast.23, bf16[1024,4096]{1,0:T(8,128)(2,1)} %bitcast.1), kind=kOutput, calls=%fused_computation.6 | convolution fusion | flops 17179869184 | bytes 33554432 | tf_op jit(solution)/shard_map/dot_general | solution.py:29
  168.7 9.3 %copy.16 = f32[1024,8,256]{2,1,0:T(8,128)} copy(f32[1024,8,256]{0,2,1:T(8,128)} %bitcast.24) | data formatting | bytes 16777216 | tf_op jit(solution)/shard_map/reshape | solution.py:33
  178.0 101.2 %all_to_all.23 = f32[1024,8,256]{2,1,0:T(8,128)S(1)} all-to-all(f32[1024,8,256]{2,1,0:T(8,128)} %copy.16), channel_id=1, replica_groups=mesh['pair'=16,'virt'=8] {'pair'}, dimensions={0} | all-to-all | bytes 16777216 | tf_op jit(solution)/shard_map/all_to_all | solution.py:32
  279.2 8.1 %copy.17 = f32[64,8,16,256]{3,2,0,1:T(8,128)} copy(f32[64,8,16,256]{3,1,0,2:T(8,128)S(1)} %bitcast.22) | data formatting | bytes 16777216 | tf_op jit(solution)/shard_map/all_to_all | solution.py:32
  287.3 9.4 %all_to_all.20 = f32[64,8,4096]{2,0,1:T(8,128)} reshape(f32[64,8,16,256]{3,2,0,1:T(8,128)} %copy.17) | data formatting | bytes 16777216 | tf_op jit(solution)/shard_map/all_to_all | solution.py:32
  296.7 0.0 copy-start.3
  296.7 0.0 copy-start.4
  296.7 0.0 copy-start.1
  296.7 0.0 reduce-scatter.2.cloned.1.call-update
  296.7 0.6 copy-done.3
  297.3 0.0 copy-done.4
  297.3 0.2 select_reduce_fusion
  297.5 50.6 %reduce-scatter.2.cloned.1.call-done = f32[64,1,4096]{2,0,1:T(8,128)} async-done(((f32[64,8,4096]{2,0,1:T(8,128)}), f32[64,1,4096]{2,0,1:T(8,128)}) %reduce-scatter.2.cloned.1.call-update) | async-done | bytes 1048592 | tf_op jit(solution)/shard_map/reduce_scatter | solution.py:35
  348.2 0.0 copy-done
  348.2 0.0 copy-done.1
  348.2 6.4 %divide_convert_fusion = (bf16[64,4096]{1,0:T(8,128)(2,1)}, f32[64,4096]{1,0:T(8,128)}) fusion(f32[64]{0:T(128)S(1)} %select_reduce_fusion, f32[4096]{0:T(1024)S(1)} %copy-done.1, bf16[64,1024]{1,0:T(8,128)(2,1)S(1)} %copy-done, bf16[1024,4096]{1,0:T(8,128)(2,1)} %bitcast.1, f32[64,1,4096]{2,0,1:T(8,128)} %reduce-scatter.2.cloned.1.call-done), kind=kOutput, calls=%fused_computation.1 | convolution fusion | flops 537919488 | bytes 11157760 | tf_op jit(solution)/shard_map/dot_general | solution.py:30
Async XLA Ops:
  7.2 341.0 %copy-start = (bf16[64,1024]{1,0:T(8,128)(2,1)S(1)}, bf16[64,1024]{1,0:T(8,128)(2,1)}, u32[]{:S(2)}) copy-start(bf16[64,1024]{1,0:T(8,128)(2,1)} %param.9) | copy-start | bytes 393220
  12.5 8.8 %copy-start.2 = (s32[256]{0:T(256)S(1)}, s32[256]{0:T(256)}, u32[]{:S(2)}) copy-start(s32[256]{0:T(256)} %param.10) | copy-start | bytes 3076
  12.5 131.9 %all-to-all-start = ((bf16[16,64,4096]{2,1,0:T(8,128)(2,1)}), bf16[16,64,4096]{2,1,0:T(8,128)(2,1)}, u32[]{:S(2)}, u32[]{:S(2)}) async-start(bf16[16,64,4096]{2,1,0:T(8,128)(2,1)} %stack.2), calls=%async_computation | async-start | bytes 16777216 | tf_op jit(solution)/shard_map/all_to_all | solution.py:27
  21.3 326.8 %reduce-scatter.2.cloned.1.call-start = ((), (), s32[]{:S(2)}) async-start(), calls=%async_computation.3 | async-start | bytes 9437184 | tf_op jit(solution)/shard_map/reduce_scatter | solution.py:35
  296.7 0.7 copy-start.3
  296.7 0.7 copy-start.4
  296.7 51.5 %copy-start.1 = (f32[4096]{0:T(1024)S(1)}, f32[4096]{0:T(1024)}, u32[]{:S(2)}) copy-start(f32[4096]{0:T(1024)} %param.13) | copy-start | bytes 49156
Sparse Core Ops, SparseCore 0:
  296.8 51.3 reduce-scatter.1
